TPU v7x, 32 devices: a whole 2x2x4 slice. The times are simulated.
32 devices in a mesh: dp: 8 (over z, x), tensor: 4 (over y, core).
Axes of the slice: x: 2, y: 2, z: 4, core: 2. Of those that a mesh axis runs over, the one named last changes fastest.
Arguments:
- activations: bfloat16 [2, 32, 256, 4096], P(None, 'dp', None, 'tensor'), may hold values from -6 to 6
- out_grads: bfloat16 [2, 32, 256, 4096], P(None, 'dp', None, 'tensor'), may hold values from -6 to 6
- proj_in: bfloat16 [2, 4096, 64], P(None, 'tensor'), may hold values from -0.09375 to 0.09375
- proj_out: bfloat16 [2, 4096, 64], P(None, 'tensor'), may hold values from -0.09375 to 0.09375
- lengths: int32 [32], P('dp'), may hold values from 32 to 256, as said below
- test_feats: bfloat16 [2, 2048, 4096], P(None, 'dp'), may hold values from -0.0059814453 to 0.0059814453
- test_slot: int32 [2048], P('dp'), may hold values from 0 to 255, as said below
Outputs:
- scores: float32 [32, 1024], P('dp')
Inputs may be any that keep to these rules, and one draw needn't show every extreme that they name: Positions from lengths[e] on are padding; some example has exactly 256 real tokens and some exactly 32. `test_slot`: within each aligned block of 256 test items a permutation of 0 to 255.
All inputs are finite; a program needn't handle non-finite values.
Results may differ from a plain program's by a relative error of at most 0.005.
Values may be sent and summed in bfloat16 or wider, within the bound.
A program may use at most 128 MiB of HBM per device.

v0:
```python
import jax
import jax.numpy as jnp
from jax import lax
from jax.sharding import PartitionSpec as P

STEPS = 4


def from_behind(value, axis, steps):
    count = lax.axis_size(axis)
    pairs = [(source, (source + steps) % count) for source in range(count)]
    return lax.ppermute(value, axis, pairs)


def score_tile(feat_rows, test_block):
    return jnp.einsum("lef,ltf->et", feat_rows, test_block, preferred_element_type=jnp.float32)


def shards(activations, out_grads, proj_in, proj_out, lengths, test_feats, test_slot):
    low_rank = proj_in.shape[2]
    part_act = jnp.einsum(
        "lesd,ldr->lesr", activations, proj_in, preferred_element_type=jnp.float32
    )
    part_grad = jnp.einsum(
        "lesd,ldr->lesr", out_grads, proj_out, preferred_element_type=jnp.float32
    )
    partial_proj = jnp.concatenate([part_act, part_grad], axis=3)
    summed = lax.psum(partial_proj, "tensor")
    layer_count, example_count, token_count = (summed.shape[0], summed.shape[1], summed.shape[2])
    rounded = summed.astype(jnp.bfloat16)
    positions = jnp.arange(token_count, dtype=jnp.int32)
    kept_mask = (positions[None, :] < lengths[:, None]).astype(jnp.bfloat16)
    grad_side = rounded[..., low_rank:] * kept_mask[None, :, :, None]
    outer_sums = jnp.einsum(
        "lesa,lesb->leab", grad_side, rounded[..., :low_rank], preferred_element_type=jnp.float32
    )
    outer_sums = outer_sums.reshape(layer_count, example_count, low_rank * low_rank)
    features = outer_sums.astype(jnp.bfloat16)
    ordered = jnp.zeros_like(test_feats).at[:, test_slot, :].set(test_feats)
    score_tiles = [score_tile(features, ordered)]
    for distance in range(1, STEPS):
        visiting = from_behind(features, "dp", -distance)
        returned = from_behind(score_tile(visiting, ordered), "dp", distance)
        score_tiles.append(returned)
    return jnp.concatenate(score_tiles, axis=1)


def solution(mesh):
    return jax.shard_map(
        shards,
        mesh=mesh,
        in_specs=(
            P(None, "dp", None, "tensor"),
            P(None, "dp", None, "tensor"),
            P(None, "tensor", None),
            P(None, "tensor", None),
            P("dp"),
            P(None, "dp", None),
            P("dp"),
        ),
        out_specs=P("dp", None),
        check_vma=False,
    )
```

profile of v0, /device:TPU:0, one launch (start us, length us, event | category | flops | bytes accessed | tf_op | source)
XLA Modules:
  0.0 108.4 jit_solution(12648357441231328048)
XLA Ops:
  0.0 0.9 copy-done
  1.0 4.0 %fusion.21 = f32[2,4,256,64]{2,3,1,0:T(8,128)S(1)} fusion(bf16[2,4,256,1024]{3,2,1,0:T(8,128)(2,1)} %param.8, bf16[2,1024,64]{1,2,0:T(8,128)(2,1)S(1)} %copy-done), kind=kOutput, calls=%fused_computation.17 | convolution fusion | flops 268435456 | bytes 4980736 | tf_op jit(solution)/shard_map/lesd,ldr->lesr/dot_general | solution.py:24
  5.0 0.0 copy-start.5
  5.0 0.0 copy-start.4
  5.0 1.4 %fusion.23 = f32[2,4,256,64]{2,3,1,0:T(8,128)S(1)} fusion(bf16[2,4,256,1024]{3,2,1,0:T(8,128)(2,1)S(1)} %copy-done.2, bf16[2,1024,64]{1,2,0:T(8,128)(2,1)S(1)} %copy-done.3), kind=kOutput, calls=%fused_computation.19 | convolution fusion | flops 268435456 | bytes 4980736 | tf_op jit(solution)/shard_map/lesd,ldr->lesr/dot_general | solution.py:21
  6.4 0.1 pad_maximum_fusion
  6.5 28.0 %all-reduce.1 = bf16[2,4,256,128]{2,3,1,0:T(8,128)(2,1)S(1)} all-reduce(f32[2,4,256,128]{2,3,1,0:T(8,128)S(1)} %pad_maximum_fusion), channel_id=1, replica_groups=mesh['dp'=8,'tensor'=4] {'tensor'}, use_global_device_ids=true, to_apply=%region_0.0 | all-reduce | flops 262144 | bytes 1572864 | tf_op jit(solution)/shard_map/psum | solution.py:28
  34.5 0.0 copy-done.5
  34.5 0.1 fusion.26
  34.6 0.2 convolution_convert_fusion
  34.8 0.1 convert_element_type.19
  35.0 4.6 %collective-permute-start = (bf16[2,4,4096]{2,1,0:T(4,128)(2,1)S(1)}, bf16[2,4,4096]{2,1,0:T(4,128)(2,1)S(1)}, u32[]{:S(2)}, u32[]{:S(2)}) collective-permute-start(bf16[2,4,4096]{2,1,0:T(4,128)(2,1)S(1)} %convert_element_type.19), channel_id=1, source_target_pairs={{0,28},{4,0},{8,4},{12,8},{16,12},{20,16},{24,20},{28,24},{1,29},{... | collective-permute-start | bytes 196616 | tf_op jit(solution)/shard_map/ppermute | solution.py:12
  39.6 0.4 collective-permute-start.2
  40.0 0.0 collective-permute-start.4
  40.0 8.6 %copy.8 = bf16[256,2,4096]{2,1,0:T(2,128)(2,1)} copy(bf16[256,2,4096]{2,0,1:T(8,128)(2,1)} %bitcast.27) | data formatting | bytes 8388608 | tf_op args[5]
  48.6 6.2 %broadcast_in_dim.4 = bf16[2,256,4096]{2,0,1:T(2,128)(2,1)} broadcast(bf16[]{:T(256)} %constant.0.clone.1), dimensions={} | broadcast | bytes 4194306 | tf_op jit(solution)/shard_map/broadcast_in_dim | solution.py:39
  54.8 34.5 %scatter_fusion = bf16[2,256,4096]{2,0,1:T(2,128)(2,1)} fusion(bf16[2,256,4096]{2,0,1:T(2,128)(2,1)} %broadcast_in_dim.4, s32[256]{0:T(256)S(1)} %compare_select_fusion, bf16[256,2,4096]{2,1,0:T(2,128)(2,1)} %copy.8), kind=kCustom, calls=%fused_computation | custom fusion | bytes 12583936 | tf_op jit(solution)/shard_map/scatter | solution.py:39
  89.3 0.0 collective-permute-done
  89.3 4.7 %fusion.11 = f32[4,256]{1,0:T(4,128)S(1)} fusion(bf16[2,4,4096]{2,1,0:T(4,128)(2,1)S(1)} %collective-permute-done, bf16[2,256,4096]{2,0,1:T(2,128)(2,1)} %scatter_fusion), kind=kOutput, calls=%fused_computation.11 | convolution fusion | flops 16777216 | bytes 4263936 | tf_op jit(solution)/shard_map/lef,ltf->et/dot_general | solution.py:16
  94.0 2.1 %collective-permute-start.1 = (f32[4,256]{1,0:T(4,128)S(1)}, f32[4,256]{1,0:T(4,128)S(1)}, u32[]{:S(2)}, u32[]{:S(2)}) collective-permute-start(f32[4,256]{1,0:T(4,128)S(1)} %fusion.11), channel_id=1, source_target_pairs={{0,4},{4,8},{8,12},{12,16},{16,20},{20,24},{24,28},{28,0},{1,5},{5... | collective-permute-start | bytes 12296 | tf_op jit(solution)/shard_map/ppermute | solution.py:12
  96.1 0.0 collective-permute-done.2
  96.1 0.0 copy-done.1
  96.1 2.3 %fusion.14 = f32[4,256]{1,0:T(4,128)S(1)} fusion(bf16[2,4,4096]{2,1,0:T(4,128)(2,1)S(1)} %collective-permute-done.2, bf16[2,256,4096]{2,0,1:T(2,128)(2,1)S(1)} %copy-done.1), kind=kOutput, calls=%fused_computation.12 | convolution fusion | flops 16777216 | bytes 4263936 | tf_op jit(solution)/shard_map/lef,ltf->et/dot_general | solution.py:16
  98.5 1.6 %collective-permute-start.3 = (f32[4,256]{1,0:T(4,128)S(1)}, f32[4,256]{1,0:T(4,128)S(1)}, u32[]{:S(2)}, u32[]{:S(2)}) collective-permute-start(f32[4,256]{1,0:T(4,128)S(1)} %fusion.14), channel_id=1, source_target_pairs={{0,8},{4,12},{8,16},{12,20},{16,24},{20,28},{24,0},{28,4},{1,9},{5... | collective-permute-start | bytes 12296 | tf_op jit(solution)/shard_map/ppermute | solution.py:12
  100.0 0.0 collective-permute-done.4
  100.0 2.3 %fusion.17 = f32[4,256]{1,0:T(4,128)S(1)} fusion(bf16[2,4,4096]{2,1,0:T(4,128)(2,1)S(1)} %collective-permute-done.4, bf16[2,256,4096]{2,0,1:T(2,128)(2,1)S(1)} %copy-done.1), kind=kOutput, calls=%fused_computation.13 | convolution fusion | flops 16777216 | bytes 4263936 | tf_op jit(solution)/shard_map/lef,ltf->et/dot_general | solution.py:16
  102.4 1.1 %collective-permute-start.5 = (f32[4,256]{1,0:T(4,128)S(1)}, f32[4,256]{1,0:T(4,128)S(1)}, u32[]{:S(2)}, u32[]{:S(2)}) collective-permute-start(f32[4,256]{1,0:T(4,128)S(1)} %fusion.17), channel_id=1, source_target_pairs={{0,12},{4,16},{8,20},{12,24},{16,28},{20,0},{24,4},{28,8},{1,13},{... | collective-permute-start | bytes 12296 | tf_op jit(solution)/shard_map/ppermute | solution.py:12
  103.5 2.3 %fusion.8 = f32[4,256]{1,0:T(4,128)S(1)} fusion(bf16[2,4,4096]{2,1,0:T(4,128)(2,1)S(1)} %convert_element_type.19, bf16[2,256,4096]{2,0,1:T(2,128)(2,1)S(1)} %copy-done.1), kind=kOutput, calls=%fused_computation.10 | convolution fusion | flops 16777216 | bytes 4263936 | tf_op jit(solution)/shard_map/lef,ltf->et/dot_general | solution.py:16
  105.8 0.0 collective-permute-done.1
  105.8 0.0 collective-permute-done.3
  105.8 1.9 %collective-permute-done.5 = f32[4,256]{1,0:T(4,128)S(1)} collective-permute-done((f32[4,256]{1,0:T(4,128)S(1)}, f32[4,256]{1,0:T(4,128)S(1)}, u32[]{:S(2)}, u32[]{:S(2)}) %collective-permute-start.5) | collective-permute-done | bytes 4128 | tf_op jit(solution)/shard_map/ppermute | solution.py:12
  107.8 0.6 pad_maximum_fusion.1
  (8 shorter events, 0.0 us)
Async XLA Ops:
  0.0 1.0 copy-start
  0.0 5.0 %copy-start.2 = (bf16[2,4,256,1024]{3,2,1,0:T(8,128)(2,1)S(1)}, bf16[2,4,256,1024]{3,2,1,0:T(8,128)(2,1)}, u32[]{:S(2)}) copy-start(bf16[2,4,256,1024]{3,2,1,0:T(8,128)(2,1)} %param.7) | copy-start | bytes 12582916
  0.0 5.0 %copy-start.3 = (bf16[2,1024,64]{1,2,0:T(8,128)(2,1)S(1)}, bf16[2,1024,64]{1,2,0:T(8,128)(2,1)}, u32[]{:S(2)}) copy-start(bf16[2,1024,64]{1,2,0:T(8,128)(2,1)} %param.9) | copy-start | bytes 786436
  5.0 29.5 %copy-start.5 = (s32[4]{0:T(128)S(1)}, s32[4]{0:T(128)}, u32[]{:S(2)}) copy-start(s32[4]{0:T(128)} %param.11) | copy-start | bytes 52
  5.0 35.0 %copy-start.4 = (s32[256]{0:T(256)S(1)}, s32[256]{0:T(256)}, u32[]{:S(2)}) copy-start(s32[256]{0:T(256)} %param.13) | copy-start | bytes 3076
  35.0 54.3 %collective-permute-start = (bf16[2,4,4096]{2,1,0:T(4,128)(2,1)S(1)}, bf16[2,4,4096]{2,1,0:T(4,128)(2,1)S(1)}, u32[]{:S(2)}, u32[]{:S(2)}) collective-permute-start(bf16[2,4,4096]{2,1,0:T(4,128)(2,1)S(1)} %convert_element_type.19), channel_id=1, source_target_pairs={{0,28},{4,0},{8,4},{12,8},{16,12},{20,16},{24,20},{28,24},{1,29},{... | collective-permute-start | bytes 196616 | tf_op jit(solution)/shard_map/ppermute | solution.py:12
  39.6 56.6 %collective-permute-start.2 = (bf16[2,4,4096]{2,1,0:T(4,128)(2,1)S(1)}, bf16[2,4,4096]{2,1,0:T(4,128)(2,1)S(1)}, u32[]{:S(2)}, u32[]{:S(2)}) collective-permute-start(bf16[2,4,4096]{2,1,0:T(4,128)(2,1)S(1)} %convert_element_type.19), channel_id=1, source_target_pairs={{0,24},{4,28},{8,0},{12,4},{16,8},{20,12},{24,16},{28,20},{1,25},{... | collective-permute-start | bytes 196616 | tf_op jit(solution)/shard_map/ppermute | solution.py:12
  40.0 60.0 %collective-permute-start.4 = (bf16[2,4,4096]{2,1,0:T(4,128)(2,1)S(1)}, bf16[2,4,4096]{2,1,0:T(4,128)(2,1)S(1)}, u32[]{:S(2)}, u32[]{:S(2)}) collective-permute-start(bf16[2,4,4096]{2,1,0:T(4,128)(2,1)S(1)} %convert_element_type.19), channel_id=1, source_target_pairs={{0,20},{4,24},{8,28},{12,0},{16,4},{20,8},{24,12},{28,16},{1,21},{... | collective-permute-start | bytes 196616 | tf_op jit(solution)/shard_map/ppermute | solution.py:12
  89.3 6.8 %copy-start.1 = (bf16[2,256,4096]{2,0,1:T(2,128)(2,1)S(1)}, bf16[2,256,4096]{2,0,1:T(2,128)(2,1)}, u32[]{:S(2)}) copy-start(bf16[2,256,4096]{2,0,1:T(2,128)(2,1)} %scatter_fusion) | copy-start | bytes 12582916
  94.0 11.8 %collective-permute-start.1 = (f32[4,256]{1,0:T(4,128)S(1)}, f32[4,256]{1,0:T(4,128)S(1)}, u32[]{:S(2)}, u32[]{:S(2)}) collective-permute-start(f32[4,256]{1,0:T(4,128)S(1)} %fusion.11), channel_id=1, source_target_pairs={{0,4},{4,8},{8,12},{12,16},{16,20},{20,24},{24,28},{28,0},{1,5},{5... | collective-permute-start | bytes 12296 | tf_op jit(solution)/shard_map/ppermute | solution.py:12
  98.5 7.4 %collective-permute-start.3 = (f32[4,256]{1,0:T(4,128)S(1)}, f32[4,256]{1,0:T(4,128)S(1)}, u32[]{:S(2)}, u32[]{:S(2)}) collective-permute-start(f32[4,256]{1,0:T(4,128)S(1)} %fusion.14), channel_id=1, source_target_pairs={{0,8},{4,12},{8,16},{12,20},{16,24},{20,28},{24,0},{28,4},{1,9},{5... | collective-permute-start | bytes 12296 | tf_op jit(solution)/shard_map/ppermute | solution.py:12
  102.4 5.4 %collective-permute-start.5 = (f32[4,256]{1,0:T(4,128)S(1)}, f32[4,256]{1,0:T(4,128)S(1)}, u32[]{:S(2)}, u32[]{:S(2)}) collective-permute-start(f32[4,256]{1,0:T(4,128)S(1)} %fusion.17), channel_id=1, source_target_pairs={{0,12},{4,16},{8,20},{12,24},{16,28},{20,0},{24,4},{28,8},{1,13},{... | collective-permute-start | bytes 12296 | tf_op jit(solution)/shard_map/ppermute | solution.py:12
where the time goes:
time: 109 us; the launch traced here: 108 us
  local copies, waits for them, and re-layouts  50.4 us (46%)
  blocking collectives  28 us (26%)
  matrix products  17.3 us (16%)
  starting transfers between devices  9.84 us (9%)
  waiting for transfers between devices  1.95 us (2%)
    scatter x1, local copies, waits for them, and re-layouts, shards(): ordered = jnp.zeros_like(test_feats).at[:, test_slot, :].set(test_feats)  34.5 us
    psum x1, blocking collectives, shards(): summed = lax.psum(partial_proj, 'tensor')  28 us
    dot_general x4, matrix products, score_tile(): jnp.einsum('lef,ltf->et', feat_rows, test_block, preferred_element_type=j...  11.7 us
    ppermute x6, starting transfers between devices, from_behind(): return lax.ppermute(value, axis, pairs)  9.84 us
    unnamed x13, local copies, waits for them, and re-layouts  9.55 us
    broadcast_in_dim x1, local copies, waits for them, and re-layouts, shards(): ordered = jnp.zeros_like(test_feats).at[:, test_slot, :].set(test_feats)  6.19 us
    dot_general x1, matrix products, shards(): jnp.einsum('lesd,ldr->lesr', out_grads, proj_out, preferred_element_type=...  4.03 us
  transfers between devices with their start and end apart: 6, of which 1 were waited for; matrix products, arithmetic and copies ran while one was open for 56% of the time, Pallas kernels for 0%

commit v1 on v0

v1 whole, which is shorter than its diff:
```python
import functools

import jax
import jax.numpy as jnp
from jax import lax
from jax.experimental import pallas as pl
from jax.experimental.pallas import tpu as pltpu
from jax.sharding import PartitionSpec as P

STEPS = 4
LANES = 128
WIRE = jnp.float32
MESH = pl.DeviceIdType.MESH


def kernel(
    n_dp, n_t, examples, seq, plan,
    act, grad, win, wout, lens, tests, slot,
    out,
    abuf, gbuf, wpad, tbuf, ordered, msend, mrecv, own, ysend, yrecv,
    fscr, fsend, frecv, flat, ssend, srecv,
    in_sem, w_sem, t_sem, m_send, m_recv, y_send, y_recv, f_send, f_recv, s_send, s_recv,
):
    unit, n_unit, n_chip, rank = plan
    d, t = lax.axis_index("dp"), lax.axis_index("tensor")
    chip, core = t // 2, t % 2
    depth = act.shape[1]
    layer_rows = examples * seq
    rank_rows = rank * rank // LANES
    mate = {"dp": d, "tensor": 2 * chip + 1 - core}

    def row_of(chip_index, core_index, u):
        return ((2 * chip_index + core_index) * n_unit + u) * unit

    steps = [(o, u) for o in list(range(1, n_chip)) + [0] for u in range(n_unit)]
    units = []
    for o, u in steps:
        where = lax.rem(chip + o, n_chip)
        units.append(row_of(where, 1 - core, u))
        units.append(row_of(where, core, u))

    layers = win.shape[0]
    w_copies = []
    for layer in range(layers):
        w_copies.append(pltpu.make_async_copy(win.at[layer], wpad.at[layer, :rank, :depth], w_sem.at[2 * layer]))
        w_copies.append(pltpu.make_async_copy(wout.at[layer], wpad.at[layer, rank:, depth:], w_sem.at[2 * layer + 1]))
    in_copies = []
    for i, row in enumerate(units):
        rows = pl.ds(pl.multiple_of(row, unit), unit)
        in_copies.append((
            pltpu.make_async_copy(act.at[rows], abuf.at[i], in_sem.at[2 * i]),
            pltpu.make_async_copy(grad.at[rows], gbuf.at[i], in_sem.at[2 * i + 1]),
        ))
    my_row = row_of(chip, core, 0)
    my_layer = my_row // layer_rows
    t_copy = pltpu.make_async_copy(tests.at[my_layer], tbuf, t_sem)
    for copy in w_copies:
        copy.start()
    for pair in in_copies:
        pair[0].start()
        pair[1].start()
    t_copy.start()

    barrier = pltpu.get_barrier_semaphore()
    near = sorted({delta % n_dp for delta in range(1 - STEPS, STEPS)})
    for delta in near:
        for o in range(n_t):
            if delta or o:
                pl.semaphore_signal(
                    barrier, inc=1, device_id_type=MESH,
                    device_id={"dp": lax.rem(d + delta, n_dp), "tensor": lax.rem(t + o, n_t)},
                )

    empty = jnp.zeros((rank, depth), wpad.dtype)
    for layer in range(layers):
        wpad[layer, :rank, depth:] = empty
        wpad[layer, rank:, :depth] = empty
    for copy in w_copies:
        copy.wait()

    def project(i):
        for copy in in_copies[i]:
            copy.wait()
        layer = units[i] // layer_rows
        last = (((1,), (1,)), ((), ()))
        return lax.dot_general(
            abuf[i], wpad[layer, :, :depth], last, preferred_element_type=jnp.float32
        ) + lax.dot_general(gbuf[i], wpad[layer, :, depth:], last, preferred_element_type=jnp.float32)

    sends = []
    y_copies = {}
    for s, (o, u) in enumerate(steps):
        msend[s] = project(2 * s)
        if s == 0:
            pl.semaphore_wait(barrier, len(near) * n_t - 1)
        to_mate = pltpu.make_async_remote_copy(
            src_ref=msend.at[s], dst_ref=mrecv.at[s], send_sem=m_send.at[s], recv_sem=m_recv.at[s],
            device_id=mate, device_id_type=MESH,
        )
        to_mate.start()
        sends.append(to_mate)
        own[s] = project(2 * s + 1)
        to_mate.wait_recv()
        if o == 0:
            continue
        slot_of = (o - 1) * n_unit + u
        ysend[slot_of] = (own[s] + mrecv[s]).astype(ysend.dtype)
        across = pltpu.make_async_remote_copy(
            src_ref=ysend.at[slot_of], dst_ref=yrecv.at[slot_of],
            send_sem=y_send.at[slot_of], recv_sem=y_recv.at[slot_of],
            device_id={"dp": d, "tensor": 2 * lax.rem(chip + o, n_chip) + core}, device_id_type=MESH,
        )
        across.start()
        sends.append(across)
        y_copies[o, u] = across

    items = tbuf.shape[0]
    t_copy.wait()
    place = jnp.where(
        lax.broadcasted_iota(jnp.int32, (items, items), 0) == jnp.broadcast_to(slot[...], (items, items)), 1.0, 0.0
    ).astype(tbuf.dtype)
    wide = 2 * LANES

    def put(b, carry):
        columns = pl.ds(pl.multiple_of(b * wide, wide), wide)
        ordered[:, columns] = jnp.dot(place, tbuf[:, columns], preferred_element_type=jnp.float32).astype(ordered.dtype)
        return carry

    lax.fori_loop(0, tbuf.shape[1] // wide, put, 0)

    lane = lax.broadcasted_iota(jnp.int32, (unit, LANES), 1)
    token = lax.broadcasted_iota(jnp.int32, (unit, LANES), 0)
    lane_of = lax.broadcasted_iota(jnp.int32, (rank_rows, LANES), 1)
    for u in range(n_unit):
        s = (n_chip - 1) * n_unit + u
        total = own[s] + mrecv[s]
        for o in range(1, n_chip):
            y_copies[o, u].wait_recv()
            total = total + yrecv[(o - 1) * n_unit + u].astype(jnp.float32)
        row = row_of(chip, core, u)
        example = lax.rem(row, layer_rows) // seq
        kept = token + lax.rem(row, seq) < lens[example]
        total = jnp.where(kept, total, 0.0).astype(jnp.bfloat16).astype(jnp.float32)
        twice = jnp.where(lane < rank, total, pltpu.roll(total, rank, 1))
        outer = lax.dot_general(
            total.astype(jnp.bfloat16), twice.astype(jnp.bfloat16), (((0,), (0,)), ((), ())),
            preferred_element_type=jnp.float32,
        )
        fscr[u] = outer[rank:, :]
        even = fscr[u, pl.ds(0, rank_rows, stride=2), :]
        odd = fscr[u, pl.ds(1, rank_rows, stride=2), :]
        fsend[u] = jnp.where(lane_of < rank, even, odd).astype(jnp.bfloat16)

    feat_copies = []
    for r in range(1, STEPS):
        copy = pltpu.make_async_remote_copy(
            src_ref=fsend, dst_ref=frecv.at[r - 1], send_sem=f_send.at[r - 1], recv_sem=f_recv.at[r - 1],
            device_id={"dp": lax.rem(d + n_dp - r, n_dp), "tensor": t}, device_id_type=MESH,
        )
        copy.start()
        feat_copies.append(copy)
        sends.append(copy)

    filled = STEPS * n_unit * rank_rows
    rows = flat.shape[0] // rank_rows
    if flat.shape[0] > filled:
        flat[filled:, :] = jnp.zeros((flat.shape[0] - filled, LANES), jnp.float32)
    for r in range(STEPS):
        if r:
            feat_copies[r - 1].wait_recv()
        block = fsend[...] if r == 0 else frecv[r - 1]
        for u in range(n_unit):
            at = (r * n_unit + u) * rank_rows
            flat[at:at + rank_rows, :] = block[u].astype(jnp.float32)
    feats = jnp.concatenate(
        [flat[pl.ds(i, rows, stride=rank_rows), :] for i in range(rank_rows)], axis=1
    ).astype(jnp.bfloat16)
    scores = lax.dot_general(
        feats, ordered[...], (((1,), (1,)), ((), ())), preferred_element_type=jnp.float32
    )

    halves = items // LANES
    line = lax.broadcasted_iota(jnp.int32, (halves * examples, LANES), 0)
    back = []
    for r in [*range(1, STEPS), 0]:
        tile = jnp.zeros((halves * examples, LANES), jnp.float32)
        for u in range(n_unit):
            example = lax.rem(row_of(chip, core, u), layer_rows) // seq
            for h in range(halves):
                at = r * n_unit + u
                piece = scores[at:at + 1, h * LANES:(h + 1) * LANES]
                tile = jnp.where(line == example + h * examples, jnp.broadcast_to(piece, tile.shape), tile)
        ssend[r] = tile
        for o in range(n_t):
            if r == 0 and o == 0:
                continue
            at = r * n_t + o
            copy = pltpu.make_async_remote_copy(
                src_ref=ssend.at[r], dst_ref=srecv.at[at], send_sem=s_send.at[at], recv_sem=s_recv.at[at],
                device_id={"dp": lax.rem(d + r, n_dp), "tensor": lax.rem(t + o, n_t)}, device_id_type=MESH,
            )
            copy.start()
            back.append((at, copy))
    arrived = dict(back)
    for r in range(STEPS):
        tile = ssend[0] if r == 0 else jnp.zeros((halves * examples, LANES), jnp.float32)
        for o in range(n_t):
            at = r * n_t + o
            if at in arrived:
                arrived[at].wait_recv()
                tile = tile + srecv[at]
        for h in range(halves):
            start = r * items + h * LANES
            out[:, start:start + LANES] = tile[h * examples:(h + 1) * examples, :]
    for copy in sends:
        copy.wait_send()
    for at, copy in back:
        copy.wait_send()


def shards(n_dp, n_t, activations, out_grads, proj_in, proj_out, lengths, test_feats, test_slot):
    layers, examples, seq, depth = activations.shape
    rank = proj_in.shape[2]
    items, feat = test_feats.shape[1:]
    rows = layers * examples * seq
    chunk = rows // n_t
    unit = min(chunk, seq)
    n_unit = chunk // unit
    n_chip = n_t // 2
    n_step = n_chip * n_unit
    n_far = max(1, (n_chip - 1) * n_unit)
    rank_rows = rank * rank // LANES
    flat_rows = -(-STEPS * n_unit // 8) * 8
    tile_rows = items // LANES * examples
    dma = pltpu.SemaphoreType.DMA
    bf16, f32 = jnp.bfloat16, jnp.float32
    hbm = pl.BlockSpec(memory_space=pl.ANY)
    vmem = pl.BlockSpec(memory_space=pltpu.VMEM)
    call = pl.pallas_call(
        functools.partial(kernel, n_dp, n_t, examples, seq, (unit, n_unit, n_chip, rank)),
        out_shape=jax.ShapeDtypeStruct((examples, STEPS * items), f32),
        in_specs=[hbm, hbm, hbm, hbm, pl.BlockSpec(memory_space=pltpu.SMEM), hbm, vmem],
        out_specs=vmem,
        scratch_shapes=[
            pltpu.VMEM((2 * n_step, unit, depth), bf16),
            pltpu.VMEM((2 * n_step, unit, depth), bf16),
            pltpu.VMEM((layers, LANES, 2 * depth), bf16),
            pltpu.VMEM((items, feat), bf16),
            pltpu.VMEM((items, feat), bf16),
            pltpu.VMEM((n_step, unit, LANES), f32),
            pltpu.VMEM((n_step, unit, LANES), f32),
            pltpu.VMEM((n_step, unit, LANES), f32),
            pltpu.VMEM((n_far, unit, LANES), WIRE),
            pltpu.VMEM((n_far, unit, LANES), WIRE),
            pltpu.VMEM((n_unit, rank, LANES), f32),
            pltpu.VMEM((n_unit, rank_rows, LANES), bf16),
            pltpu.VMEM((STEPS - 1, n_unit, rank_rows, LANES), bf16),
            pltpu.VMEM((flat_rows * rank_rows, LANES), f32),
            pltpu.VMEM((STEPS, tile_rows, LANES), f32),
            pltpu.VMEM((STEPS * n_t, tile_rows, LANES), f32),
            dma((4 * n_step,)),
            dma((2 * layers,)),
            dma,
            dma((n_step,)),
            dma((n_step,)),
            dma((n_far,)),
            dma((n_far,)),
            dma((STEPS - 1,)),
            dma((STEPS - 1,)),
            dma((STEPS * n_t,)),
            dma((STEPS * n_t,)),
        ],
        compiler_params=pltpu.CompilerParams(
            collective_id=0, has_side_effects=True, vmem_limit_bytes=56 * 1024 * 1024
        ),
    )
    return call(
        activations.reshape(rows, depth),
        out_grads.reshape(rows, depth),
        proj_in.swapaxes(1, 2),
        proj_out.swapaxes(1, 2),
        lengths,
        test_feats,
        test_slot.reshape(1, items),
    )


def solution(mesh):
    return jax.shard_map(
        functools.partial(shards, mesh.shape["dp"], mesh.shape["tensor"]),
        mesh=mesh,
        in_specs=(
            P(None, "dp", None, "tensor"),
            P(None, "dp", None, "tensor"),
            P(None, "tensor", None),
            P(None, "tensor", None),
            P("dp"),
            P(None, "dp", None),
            P("dp"),
        ),
        out_specs=P("dp", None),
        check_vma=False,
    )
```

time: 109 us -> 30.1 us (0.28)
  local copies, waits for them, and re-layouts: 50.4 us -> 1.32 us
  Pallas kernels: 0 us -> 28.5 us
  blocking collectives: 28 us -> 0 us
  matrix products: 17.3 us -> 0 us
  starting transfers between devices: 9.84 us -> 0 us
  waiting for transfers between devices: 1.95 us -> 0 us
    scatter x1 -> x0, local copies, waits for them, and re-layouts: 34.5 us -> none  [shards(): ordered = jnp.zeros_like(test_feats).at[:, test_slot, :].set(test_feats)]
    pallas_call x0 -> x1, Pallas kernels: none -> 28.5 us  [shards(): call(activations.reshape(rows, depth), out_grads.reshape(rows, depth), pr...]
    psum x1 -> x0, blocking collectives: 28 us -> none  [shards(): summed = lax.psum(partial_proj, 'tensor')]
    dot_general x7 -> x0, matrix products: 17.3 us -> none  [the longest x4 11.7 us: score_tile(): jnp.einsum('lef,ltf->et', feat_rows, test_block, preferred_element_type=j...]
    ppermute x6 -> x0, starting transfers between devices: 9.84 us -> none  [from_behind(): return lax.ppermute(value, axis, pairs)]
    unnamed x13 -> x1, local copies, waits for them, and re-layouts: 9.55 us -> 1.32 us
    broadcast_in_dim x1 -> x0, local copies, waits for them, and re-layouts: 6.19 us -> none  [shards(): ordered = jnp.zeros_like(test_feats).at[:, test_slot, :].set(test_feats)]
    ppermute x6 -> x0, waiting for transfers between devices: 1.95 us -> none  [from_behind(): return lax.ppermute(value, axis, pairs)]
  transfers between devices with their start and end apart: 6 -> 0, of which waited for: 1 -> 0; matrix products, arithmetic and copies ran while one was open for 56% -> 0% of each run, Pallas kernels for 0% -> 0%
where the time goes in v1:
time: 30.1 us; the launch traced here: 29.8 us
  Pallas kernels  28.5 us (95%)
  local copies, waits for them, and re-layouts  1.32 us (4%)
    pallas_call x1, Pallas kernels, shards(): call(activations.reshape(rows, depth), out_grads.reshape(rows, depth), pr...  28.5 us
    unnamed x1, local copies, waits for them, and re-layouts  1.32 us

profile of v1, /device:TPU:0, one launch (start us, length us, event | category | flops | bytes accessed | tf_op | source)
XLA Modules:
  0.0 29.8 jit_solution(9157399767784221928)
XLA Ops:
  0.0 28.5 %shard_map.73 = f32[4,1024]{1,0:T(4,128)} custom-call(bf16[2048,1024]{1,0:T(8,128)(2,1)} %bitcast.5, bf16[2048,1024]{1,0:T(8,128)(2,1)} %bitcast.6, bf16[2,64,1024]{2,1,0:T(8,128)(2,1)} %bitcast.7, bf16[2,64,1024]{2,1,0:T(8,128)(2,1)} %bitcast.8, s32[4]{0:T(128)} %lens.1, bf16[2,256,4096]{2,1,0:T(8,128)(2,1)} %tests.1, s32[1,256]{1,0:T(1,128)} %bitcast.9), custom_call_target="tpu_custom_call" | custom-call | tf_op jit(solution)/shard_map/pallas_call | solution.py:277
  28.5 1.3 %copy.9 = f32[4,1024]{1,0:T(4,128)} copy(f32[4,1024]{1,0:T(4,128)} %shard_map.73) | data formatting | bytes 32768

commit v2 on v1

--- a/solution.py
+++ b/solution.py
@@ -9,14 +9,15 @@
 
 STEPS = 4
 LANES = 128
-WIRE = jnp.float32
+WIRE = jnp.bfloat16
 MESH = pl.DeviceIdType.MESH
 
 
 def kernel(
     n_dp, n_t, examples, seq, plan,
-    act, grad, win, wout, lens, tests, slot,
+    act, grad, win, wout, lens_hbm, tests, slot_hbm,
     out,
+    lens, slot, l_sem,
     abuf, gbuf, wpad, tbuf, ordered, msend, mrecv, own, ysend, yrecv,
     fscr, fsend, frecv, flat, ssend, srecv,
     in_sem, w_sem, t_sem, m_send, m_recv, y_send, y_recv, f_send, f_recv, s_send, s_recv,
@@ -60,6 +61,9 @@
         pair[0].start()
         pair[1].start()
     t_copy.start()
+    l_copies = [pltpu.make_async_copy(lens_hbm, lens, l_sem.at[0]), pltpu.make_async_copy(slot_hbm, slot, l_sem.at[1])]
+    for copy in l_copies:
+        copy.start()
 
     barrier = pltpu.get_barrier_semaphore()
     near = sorted({delta % n_dp for delta in range(1 - STEPS, STEPS)})
@@ -89,7 +93,24 @@
 
     sends = []
     y_copies = {}
-    for s, (o, u) in enumerate(steps):
+    to_mates = []
+
+    def pass_on(s):
+        o, u = steps[s]
+        if o == 0:
+            return
+        to_mates[s].wait_recv()
+        at = (o - 1) * n_unit + u
+        ysend[at] = (own[s] + mrecv[s]).astype(ysend.dtype)
+        across = pltpu.make_async_remote_copy(
+            src_ref=ysend.at[at], dst_ref=yrecv.at[at], send_sem=y_send.at[at], recv_sem=y_recv.at[at],
+            device_id={"dp": d, "tensor": 2 * lax.rem(chip + o, n_chip) + core}, device_id_type=MESH,
+        )
+        across.start()
+        sends.append(across)
+        y_copies[o, u] = across
+
+    for s in range(len(steps)):
         msend[s] = project(2 * s)
         if s == 0:
             pl.semaphore_wait(barrier, len(near) * n_t - 1)
@@ -98,24 +119,16 @@
             device_id=mate, device_id_type=MESH,
         )
         to_mate.start()
+        to_mates.append(to_mate)
         sends.append(to_mate)
+        if s:
+            pass_on(s - 1)
         own[s] = project(2 * s + 1)
-        to_mate.wait_recv()
-        if o == 0:
-            continue
-        slot_of = (o - 1) * n_unit + u
-        ysend[slot_of] = (own[s] + mrecv[s]).astype(ysend.dtype)
-        across = pltpu.make_async_remote_copy(
-            src_ref=ysend.at[slot_of], dst_ref=yrecv.at[slot_of],
-            send_sem=y_send.at[slot_of], recv_sem=y_recv.at[slot_of],
-            device_id={"dp": d, "tensor": 2 * lax.rem(chip + o, n_chip) + core}, device_id_type=MESH,
-        )
-        across.start()
-        sends.append(across)
-        y_copies[o, u] = across
+    pass_on(len(steps) - 1)
 
     items = tbuf.shape[0]
-    t_copy.wait()
+    for copy in [t_copy, *l_copies]:
+        copy.wait()
     place = jnp.where(
         lax.broadcasted_iota(jnp.int32, (items, items), 0) == jnp.broadcast_to(slot[...], (items, items)), 1.0, 0.0
     ).astype(tbuf.dtype)
@@ -133,6 +146,7 @@
     lane_of = lax.broadcasted_iota(jnp.int32, (rank_rows, LANES), 1)
     for u in range(n_unit):
         s = (n_chip - 1) * n_unit + u
+        to_mates[s].wait_recv()
         total = own[s] + mrecv[s]
         for o in range(1, n_chip):
             y_copies[o, u].wait_recv()
@@ -239,9 +253,12 @@
     call = pl.pallas_call(
         functools.partial(kernel, n_dp, n_t, examples, seq, (unit, n_unit, n_chip, rank)),
         out_shape=jax.ShapeDtypeStruct((examples, STEPS * items), f32),
-        in_specs=[hbm, hbm, hbm, hbm, pl.BlockSpec(memory_space=pltpu.SMEM), hbm, vmem],
+        in_specs=[hbm] * 7,
         out_specs=vmem,
         scratch_shapes=[
+            pltpu.SMEM((examples,), jnp.int32),
+            pltpu.VMEM((1, items), jnp.int32),
+            dma((2,)),
             pltpu.VMEM((2 * n_step, unit, depth), bf16),
             pltpu.VMEM((2 * n_step, unit, depth), bf16),
             pltpu.VMEM((layers, LANES, 2 * depth), bf16),

time: 30.1 us -> 27.8 us (0.924)
  Pallas kernels: 28.5 us -> 26.2 us
    pallas_call x1, Pallas kernels: 28.5 us -> 26.2 us  [shards(): call(activations.reshape(rows, depth), out_grads.reshape(rows, depth), pr...]
where the time goes in v2:
time: 27.8 us; the launch traced here: 27.6 us
  Pallas kernels  26.2 us (94%)
  local copies, waits for them, and re-layouts  1.32 us (5%)
    pallas_call x1, Pallas kernels, shards(): call(activations.reshape(rows, depth), out_grads.reshape(rows, depth), pr...  26.2 us
    unnamed x1, local copies, waits for them, and re-layouts  1.32 us

profile of v2, /device:TPU:0, one launch (start us, length us, event | category | flops | bytes accessed | tf_op | source)
XLA Modules:
  0.0 27.6 jit_solution(12126055230925159693)
XLA Ops:
  0.0 26.2 %shard_map.73 = f32[4,1024]{1,0:T(4,128)} custom-call(bf16[2048,1024]{1,0:T(8,128)(2,1)} %bitcast.5, bf16[2048,1024]{1,0:T(8,128)(2,1)} %bitcast.6, bf16[2,64,1024]{2,1,0:T(8,128)(2,1)} %bitcast.7, bf16[2,64,1024]{2,1,0:T(8,128)(2,1)} %bitcast.8, s32[4]{0:T(128)} %lens_hbm.1, bf16[2,256,4096]{2,1,0:T(8,128)(2,1)} %tests.1, s32[1,256]{1,0:T(1,128)} %bitcast.9), custom_call_target="tpu_custom_call" | custom-call | tf_op jit(solution)/shard_map/pallas_call | solution.py:294
  26.3 1.3 %copy.9 = f32[4,1024]{1,0:T(4,128)} copy(f32[4,1024]{1,0:T(4,128)} %shard_map.73) | data formatting | bytes 32768

commit v3 on v2

--- a/solution.py
+++ b/solution.py
@@ -18,7 +18,7 @@
     act, grad, win, wout, lens_hbm, tests, slot_hbm,
     out,
     lens, slot, l_sem,
-    abuf, gbuf, wpad, tbuf, ordered, msend, mrecv, own, ysend, yrecv,
+    abuf, gbuf, wpad, wturn, tbuf, ordered, msend, mrecv, own, ysend, yrecv,
     fscr, fsend, frecv, flat, ssend, srecv,
     in_sem, w_sem, t_sem, m_send, m_recv, y_send, y_recv, f_send, f_recv, s_send, s_recv,
 ):
@@ -81,15 +81,18 @@
         wpad[layer, rank:, :depth] = empty
     for copy in w_copies:
         copy.wait()
+    for layer in range(layers):
+        for b in range(2 * depth // LANES):
+            part = slice(b * LANES, (b + 1) * LANES)
+            wturn[layer, part, :] = wpad[layer, :, part].astype(jnp.float32).T.astype(wturn.dtype)
 
     def project(i):
         for copy in in_copies[i]:
             copy.wait()
         layer = units[i] // layer_rows
-        last = (((1,), (1,)), ((), ()))
-        return lax.dot_general(
-            abuf[i], wpad[layer, :, :depth], last, preferred_element_type=jnp.float32
-        ) + lax.dot_general(gbuf[i], wpad[layer, :, depth:], last, preferred_element_type=jnp.float32)
+        return jnp.dot(abuf[i], wturn[layer, :depth, :], preferred_element_type=jnp.float32) + jnp.dot(
+            gbuf[i], wturn[layer, depth:, :], preferred_element_type=jnp.float32
+        )
 
     sends = []
     y_copies = {}
@@ -262,6 +265,7 @@
             pltpu.VMEM((2 * n_step, unit, depth), bf16),
             pltpu.VMEM((2 * n_step, unit, depth), bf16),
             pltpu.VMEM((layers, LANES, 2 * depth), bf16),
+            pltpu.VMEM((layers, 2 * depth, LANES), bf16),
             pltpu.VMEM((items, feat), bf16),
             pltpu.VMEM((items, feat), bf16),
             pltpu.VMEM((n_step, unit, LANES), f32),

time: 27.8 us -> 25.7 us (0.924)
  Pallas kernels: 26.2 us -> 24.2 us
    pallas_call x1, Pallas kernels: 26.2 us -> 24.2 us  [shards(): call(activations.reshape(rows, depth), out_grads.reshape(rows, depth), pr...]
where the time goes in v3:
time: 25.7 us; the launch traced here: 25.5 us
  Pallas kernels  24.2 us (94%)
  local copies, waits for them, and re-layouts  1.32 us (5%)
    pallas_call x1, Pallas kernels, shards(): call(activations.reshape(rows, depth), out_grads.reshape(rows, depth), pr...  24.2 us
    unnamed x1, local copies, waits for them, and re-layouts  1.32 us

profile of v3, /device:TPU:0, one launch (start us, length us, event | category | flops | bytes accessed | tf_op | source)
XLA Modules:
  0.0 25.5 jit_solution(11672165770886063619)
XLA Ops:
  0.0 24.2 %shard_map.73 = f32[4,1024]{1,0:T(4,128)} custom-call(bf16[2048,1024]{1,0:T(8,128)(2,1)} %bitcast.5, bf16[2048,1024]{1,0:T(8,128)(2,1)} %bitcast.6, bf16[2,64,1024]{2,1,0:T(8,128)(2,1)} %bitcast.7, bf16[2,64,1024]{2,1,0:T(8,128)(2,1)} %bitcast.8, s32[4]{0:T(128)} %lens_hbm.1, bf16[2,256,4096]{2,1,0:T(8,128)(2,1)} %tests.1, s32[1,256]{1,0:T(1,128)} %bitcast.9), custom_call_target="tpu_custom_call" | custom-call | tf_op jit(solution)/shard_map/pallas_call | solution.py:298
  24.2 1.3 %copy.9 = f32[4,1024]{1,0:T(4,128)} copy(f32[4,1024]{1,0:T(4,128)} %shard_map.73) | data formatting | bytes 32768
